TPU v7x, 32 devices: a whole 2x2x4 slice. The times are simulated.
32 devices in a mesh: docs: 8 (over z, core), protos: 4 (over y, x).
Axes of the slice: x: 2, y: 2, z: 4, core: 2. Of those that a mesh axis runs over, the one named last changes fastest.
Arguments:
- embeddings: bfloat16 [8192, 512], P('docs'), may hold values from -12.5 to 12.5
- prototypes: bfloat16 [65536, 512], P('protos'), may hold values from -4 to 4
Outputs:
- new_prototypes: bfloat16 [65536, 512], P(('protos', 'docs'))
- column_potential: float32 [65536], P('protos')
- row_potential: float32 [8192], P('docs')
All inputs are finite; a program needn't handle non-finite values.
Results may differ from a plain program's by a relative error of at most 0.0035.
Values may be sent and summed in bfloat16 or wider, within the bound.
No kernel may reach another device: no remote copies, remote signals or barrier semaphores. Data moves between devices by JAX's collectives and lax.ppermute only.
A program may use at most 256 MiB of HBM per device.

v0:
```python
import math
import jax
import jax.numpy as jnp
from jax import lax
from jax.sharding import PartitionSpec as P

SWEEPS = 2


def on_device(embeddings, prototypes):
    local_docs = embeddings.shape[0]
    local_protos = prototypes.shape[0]
    total_docs = local_docs * lax.axis_size("docs")
    total_protos = local_protos * lax.axis_size("protos")
    logit_gain = 4.0 / math.sqrt(embeddings.shape[1])
    scores = (
        lax.dot_general(
            embeddings, prototypes, (((1,), (1,)), ((), ())), preferred_element_type=jnp.float32
        )
        * logit_gain
    )
    row_peak = lax.pmax(jnp.max(scores, axis=1), "protos")
    numerators = jnp.exp(scores - row_peak[:, None])
    row_total = lax.psum(jnp.sum(numerators, axis=1), "protos")
    rescale = 1.0
    row_scale = 1.0 / row_total
    row_weight = rescale * row_scale
    col_scale = jnp.zeros((local_protos,), jnp.float32)
    for sweep_index in range(SWEEPS):
        col_local = jnp.dot(
            row_weight,
            numerators,
            precision=lax.Precision.HIGHEST,
            preferred_element_type=jnp.float32,
        )
        col_total = lax.psum(col_local, "docs")
        col_scale = 1.0 / (total_protos * col_total)
        row_local = rescale * jnp.dot(
            numerators,
            col_scale,
            precision=lax.Precision.HIGHEST,
            preferred_element_type=jnp.float32,
        )
        row_sum = lax.psum(row_local, "protos")
        row_scale = 1.0 / (total_docs * row_sum)
        row_weight = rescale * row_scale
    column_potential = jnp.log(total_docs * col_scale)
    row_potential = jnp.log(row_scale * row_total)
    assignment = (numerators * (total_docs * row_weight)[:, None] * col_scale[None, :]).astype(
        jnp.bfloat16
    )
    summed = lax.psum_scatter(
        lax.dot_general(
            assignment, embeddings, (((0,), (0,)), ((), ())), preferred_element_type=jnp.float32
        ),
        "docs",
        scatter_dimension=0,
        tiled=True,
    )
    new_prototypes = (
        summed * lax.rsqrt(jnp.mean(summed * summed, axis=1, keepdims=True) + 1e-06)
    ).astype(jnp.bfloat16)
    return (new_prototypes, column_potential, row_potential)


def solution(mesh):
    placed = (P("docs", None), P("protos", None))
    return jax.shard_map(
        on_device,
        mesh=mesh,
        in_specs=placed,
        out_specs=(P(("protos", "docs"), None), P("protos"), P("docs")),
        check_vma=False,
    )
```

profile of v0, /device:TPU:0, one launch (start us, length us, event | category | flops | bytes accessed | tf_op | source)
XLA Modules:
  0.0 816.3 jit_solution(17064669797004932549)
XLA Ops:
  7.2 0.0 copy-start
  7.2 0.0 all-reduce.3.cloned.1.call-start
  7.2 1.2 copy-done
  8.4 31.5 %multiply_reduce_fusion = (f32[1024]{0:T(1024)S(1)}, f32[1024,16384]{1,0:T(8,128)}) fusion(bf16[1024,512]{1,0:T(8,128)(2,1)S(1)} %copy-done, bf16[16384,512]{1,0:T(8,128)(2,1)} %param.3), kind=kOutput, calls=%fused_computation.2 | convolution fusion | flops 17213423616 | bytes 84938752 | tf_op jit(solution)/shard_map/dot_general | solution.py:17
  39.9 11.3 %pmax.7 = f32[1024]{0:T(1024)S(1)} all-reduce(f32[1024]{0:T(1024)S(1)} %get-tuple-element.7), channel_id=1, replica_groups=mesh['docs'=8,'protos'=4] {'protos'}, use_global_device_ids=true, to_apply=%region_1.0 | all-reduce | flops 1024 | bytes 8192 | tf_op jit(solution)/shard_map/pmax | solution.py:22
  51.2 21.2 %fusion.7 = f32[1024]{0:T(1024)S(1)} fusion(f32[1024]{0:T(1024)S(1)} %pmax.7, f32[1024,16384]{1,0:T(8,128)} %get-tuple-element.8), kind=kLoop, calls=%fused_computation.21 | loop fusion | flops 50330624 | bytes 67117056 | tf_op jit(solution)/shard_map/reduce_sum | solution.py:24
  72.4 8.3 %psum.35 = f32[1024]{0:T(1024)S(1)} all-reduce(f32[1024]{0:T(1024)S(1)} %fusion.7), channel_id=1, replica_groups=mesh['docs'=8,'protos'=4] {'protos'}, use_global_device_ids=true, to_apply=%region_3.0 | all-reduce | flops 1024 | bytes 8192 | tf_op jit(solution)/shard_map/psum | solution.py:24
  80.7 46.4 %fusion.6 = f32[1,16384]{1,0:T(1,128)} fusion(f32[1024,1]{0,1:T(1,128)S(1)} %bitcast.20, f32[1024,16384]{1,0:T(8,128)} %get-tuple-element.8, f32[1024]{0:T(1024)S(1)} %pmax.7), kind=kOutput, calls=%fused_computation.20 | convolution fusion | flops 234881024 | bytes 67182592 | tf_op jit(solution)/shard_map/dot_general | solution.py:30
  127.1 0.0 all-reduce.3.cloned.1.call-update
  127.1 0.6 all-reduce.5.cloned.1.call-start
  127.8 53.4 %all-reduce.3.cloned.1.call-done = f32[16384]{0:T(1024)} async-done(((f32[16384]{0:T(1024)}), f32[16384]{0:T(1024)}) %all-reduce.3.cloned.1.call-update) | async-done | bytes 65552 | tf_op jit(solution)/shard_map/psum | solution.py:36
  181.2 0.9 multiply_divide_fusion.1
  182.1 69.4 %fusion.5 = f32[1,1024]{1,0:T(1,128)S(1)} fusion(f32[16384,1]{0,1:T(1,128)S(1)} %bitcast.16, f32[1024,16384]{1,0:T(8,128)} %get-tuple-element.8, f32[1024]{0:T(1024)S(1)} %pmax.7), kind=kOutput, calls=%fused_computation.19 | convolution fusion | flops 234881024 | bytes 67182592 | tf_op jit(solution)/shard_map/dot_general | solution.py:38
  251.5 10.0 %psum.37 = f32[1024]{0:T(1024)S(1)} all-reduce(f32[1024]{0:T(1024)S(1)} %bitcast.21), channel_id=1, replica_groups=mesh['docs'=8,'protos'=4] {'protos'}, use_global_device_ids=true, to_apply=%region_5.0 | all-reduce | flops 1024 | bytes 8192 | tf_op jit(solution)/shard_map/psum | solution.py:44
  261.5 46.4 %fusion.4 = f32[1,16384]{1,0:T(1,128)} fusion(f32[1024,1]{0,1:T(1,128)S(1)} %bitcast.19, f32[1024,16384]{1,0:T(8,128)} %get-tuple-element.8, f32[1024]{0:T(1024)S(1)} %pmax.7), kind=kOutput, calls=%fused_computation.18 | convolution fusion | flops 234881024 | bytes 67182592 | tf_op jit(solution)/shard_map/dot_general | solution.py:30
  307.9 0.0 all-reduce.5.cloned.1.call-update
  307.9 0.3 reduce-scatter.2.cloned.1.call-start
  308.1 50.7 %all-reduce.5.cloned.1.call-done = f32[16384]{0:T(1024)} async-done(((f32[16384]{0:T(1024)}), f32[16384]{0:T(1024)}) %all-reduce.5.cloned.1.call-update) | async-done | bytes 65552 | tf_op jit(solution)/shard_map/psum | solution.py:36
  358.8 1.5 multiply_log_fusion
  360.3 69.4 %fusion.3 = f32[1,1024]{1,0:T(1,128)S(1)} fusion(f32[16384,1]{0,1:T(1,128)S(1)} %bitcast.15, f32[1024,16384]{1,0:T(8,128)} %get-tuple-element.8, f32[1024]{0:T(1024)S(1)} %pmax.7), kind=kOutput, calls=%fused_computation.17 | convolution fusion | flops 234881024 | bytes 67182592 | tf_op jit(solution)/shard_map/dot_general | solution.py:38
  429.7 10.1 %psum.39 = f32[1024]{0:T(1024)S(1)} all-reduce(f32[1024]{0:T(1024)S(1)} %bitcast.22), channel_id=1, replica_groups=mesh['docs'=8,'protos'=4] {'protos'}, use_global_device_ids=true, to_apply=%region_7.0 | all-reduce | flops 1024 | bytes 8192 | tf_op jit(solution)/shard_map/psum | solution.py:44
  439.8 0.6 multiply_log_fusion.1
  440.4 39.8 %fusion = f32[16384,512]{1,0:T(8,128)} fusion(bf16[1024,512]{1,0:T(8,128)(2,1)S(1)} %copy-done, f32[16384]{0:T(1024)S(1)} %get-tuple-element.4, f32[1024]{0:T(1024)S(1)} %get-tuple-element.6, f32[1024,16384]{1,0:T(8,128)} %get-tuple-element.8, f32[1024]{0:T(1024)S(1)} %pmax.7), kind=kOutput, calls=%fused_computation.3 | convolution fusion | flops 17263755264 | bytes 101785600 | tf_op jit(solution)/shard_map/dot_general | solution.py:53
  480.2 0.0 reduce-scatter.2.cloned.1.call-update
  480.2 322.9 %reduce-scatter.2.cloned.1.call-done = f32[2048,512]{1,0:T(8,128)} async-done(((f32[16384,512]{1,0:T(8,128)}), f32[2048,512]{1,0:T(8,128)}) %reduce-scatter.2.cloned.1.call-update) | async-done | bytes 4194320 | tf_op jit(solution)/shard_map/reduce_scatter | solution.py:52
  803.1 2.5 multiply_reduce_fusion.1
  805.7 3.8 multiply_convert_fusion.2
  (3 shorter events, 0.0 us)
Async XLA Ops:
  7.2 1.2 copy-start
  7.2 174.0 %all-reduce.3.cloned.1.call-start = ((), (), s32[]{:S(2)}) async-start(), calls=%async_computation.1 | async-start | bytes 131072 | tf_op jit(solution)/shard_map/psum | solution.py:36
  127.1 231.7 %all-reduce.5.cloned.1.call-start = ((), (), s32[]{:S(2)}) async-start(), calls=%async_computation.2 | async-start | bytes 131072 | tf_op jit(solution)/shard_map/psum | solution.py:36
  307.9 495.2 %reduce-scatter.2.cloned.1.call-start = ((), (), s32[]{:S(2)}) async-start(), calls=%async_computation.3 | async-start | bytes 37748736 | tf_op jit(solution)/shard_map/reduce_scatter | solution.py:52
Sparse Core Ops, SparseCore 0:
  127.3 53.9 all-reduce.2
  308.0 50.7 all-reduce.4
  480.4 322.6 reduce-scatter.1
where the time goes:
time: 820 us; the launch traced here: 816 us
  waiting for transfers between devices  427 us (52%)
  matrix products  303 us (37%)
  blocking collectives  39.7 us (5%)
  other arithmetic  30.6 us (4%)
  between operations  14.1 us (2%)
    reduce_scatter x1, waiting for transfers between devices, on_device(): lax.psum_scatter(lax.dot_general(assignment, embeddings, (((0,), (0,)), (...  323 us
    dot_general x2, matrix products, on_device(): jnp.dot(numerators, col_scale, precision=lax.Precision.HIGHEST, preferred...  139 us
    psum x2, waiting for transfers between devices, on_device(): col_total = lax.psum(col_local, 'docs')  104 us
    dot_general x2, matrix products, on_device(): jnp.dot(row_weight, numerators, precision=lax.Precision.HIGHEST, preferre...  92.8 us
    dot_general x1, matrix products, on_device(): lax.dot_general(assignment, embeddings, (((0,), (0,)), ((), ())), preferr...  39.8 us
    dot_general x1, matrix products, on_device(): lax.dot_general(embeddings, prototypes, (((1,), (1,)), ((), ())), preferr...  31.5 us
    reduce_sum x1, other arithmetic, on_device(): row_total = lax.psum(jnp.sum(numerators, axis=1), 'protos')  21.2 us
    psum x2, blocking collectives, on_device(): row_sum = lax.psum(row_local, 'protos')  20.1 us
  transfers between devices with their start and end apart: 3, of which 3 were waited for; matrix products, arithmetic and copies ran while one was open for 0% of the time, Pallas kernels for 0%

commit v1 on v0

--- a/solution.py
+++ b/solution.py
@@ -33,7 +33,11 @@
             precision=lax.Precision.HIGHEST,
             preferred_element_type=jnp.float32,
         )
-        col_total = lax.psum(col_local, "docs")
+        col_total = col_local
+        for hop in (1, 2, 4):
+            col_total = col_total + lax.ppermute(
+                col_total, "docs", [(dev, dev ^ hop) for dev in range(8)]
+            )
         col_scale = 1.0 / (total_protos * col_total)
         row_local = rescale * jnp.dot(
             numerators,

time: 820 us -> 737 us (0.90)
  waiting for transfers between devices: 427 us -> 340 us
    psum x2 -> x0, waiting for transfers between devices: 104 us -> none  [on_device(): col_total = lax.psum(col_local, 'docs')]
    ppermute x0 -> x6, waiting for transfers between devices: none -> 13.1 us  [on_device(): lax.ppermute(col_total, 'docs', [(dev, dev ^ hop) for dev in range(8)])]
    ppermute x0 -> x6, starting transfers between devices: none -> 8.91 us  [on_device(): lax.ppermute(col_total, 'docs', [(dev, dev ^ hop) for dev in range(8)])]
  transfers between devices with their start and end apart: 3 -> 7, of which waited for: 3 -> 7; matrix products, arithmetic and copies ran while one was open for 0% -> 0% of each run, Pallas kernels for 0% -> 0%
where the time goes in v1:
time: 737 us; the launch traced here: 733 us
  waiting for transfers between devices  340 us (46%)
  matrix products  303 us (41%)
  blocking collectives  36.6 us (5%)
  other arithmetic  29 us (4%)
  between operations  14.4 us (2%)
  starting transfers between devices  8.95 us (1%)
    reduce_scatter x1, waiting for transfers between devices, on_device(): lax.psum_scatter(lax.dot_general(assignment, embeddings, (((0,), (0,)), (...  327 us
    dot_general x2, matrix products, on_device(): jnp.dot(numerators, col_scale, precision=lax.Precision.HIGHEST, preferred...  140 us
    dot_general x2, matrix products, on_device(): jnp.dot(row_weight, numerators, precision=lax.Precision.HIGHEST, preferre...  91.7 us
    dot_general x1, matrix products, on_device(): lax.dot_general(assignment, embeddings, (((0,), (0,)), ((), ())), preferr...  40.1 us
    dot_general x1, matrix products, on_device(): lax.dot_general(embeddings, prototypes, (((1,), (1,)), ((), ())), preferr...  31.5 us
    reduce_sum x1, other arithmetic, on_device(): row_total = lax.psum(jnp.sum(numerators, axis=1), 'protos')  21.2 us
    psum x2, blocking collectives, on_device(): row_sum = lax.psum(row_local, 'protos')  17 us
  transfers between devices with their start and end apart: 7, of which 7 were waited for; matrix products, arithmetic and copies ran while one was open for 0% of the time, Pallas kernels for 0%

profile of v1, /device:TPU:0, one launch (start us, length us, event | category | flops | bytes accessed | tf_op | source)
XLA Modules:
  0.0 733.2 jit_solution(2091199620367050467)
XLA Ops:
  7.2 0.0 copy-start
  7.2 0.0 reduce-scatter.2.cloned.1.call-start
  7.2 1.2 copy-done
  8.4 31.5 %multiply_reduce_fusion = (f32[1024]{0:T(1024)S(1)}, f32[1024,16384]{1,0:T(8,128)}) fusion(bf16[1024,512]{1,0:T(8,128)(2,1)S(1)} %copy-done, bf16[16384,512]{1,0:T(8,128)(2,1)} %param.3), kind=kOutput, calls=%fused_computation.2 | convolution fusion | flops 17213423616 | bytes 84938752 | tf_op jit(solution)/shard_map/dot_general | solution.py:17
  39.9 11.3 %pmax.7 = f32[1024]{0:T(1024)S(1)} all-reduce(f32[1024]{0:T(1024)S(1)} %get-tuple-element.7), channel_id=1, replica_groups=mesh['docs'=8,'protos'=4] {'protos'}, use_global_device_ids=true, to_apply=%region_1.0 | all-reduce | flops 1024 | bytes 8192 | tf_op jit(solution)/shard_map/pmax | solution.py:22
  51.2 21.2 %fusion.7 = f32[1024]{0:T(1024)S(1)} fusion(f32[1024]{0:T(1024)S(1)} %pmax.7, f32[1024,16384]{1,0:T(8,128)} %get-tuple-element.8), kind=kLoop, calls=%fused_computation.21 | loop fusion | flops 50330624 | bytes 67117056 | tf_op jit(solution)/shard_map/reduce_sum | solution.py:24
  72.4 8.3 %psum.21 = f32[1024]{0:T(1024)S(1)} all-reduce(f32[1024]{0:T(1024)S(1)} %fusion.7), channel_id=1, replica_groups=mesh['docs'=8,'protos'=4] {'protos'}, use_global_device_ids=true, to_apply=%region_3.0 | all-reduce | flops 1024 | bytes 8192 | tf_op jit(solution)/shard_map/psum | solution.py:24
  80.7 45.8 %fusion.6 = f32[1,16384]{1,0:T(1,128)S(1)} fusion(f32[1024,1]{0,1:T(1,128)S(1)} %bitcast.22, f32[1024,16384]{1,0:T(8,128)} %get-tuple-element.8, f32[1024]{0:T(1024)S(1)} %pmax.7), kind=kOutput, calls=%fused_computation.20 | convolution fusion | flops 234881024 | bytes 67182592 | tf_op jit(solution)/shard_map/dot_general | solution.py:30
  126.5 0.0 collective-permute-start
  126.5 1.3 collective-permute-done
  127.8 1.6 collective-permute-start.1
  129.4 2.7 collective-permute-done.1
  132.1 2.7 collective-permute-start.2
  134.8 2.6 collective-permute-done.2
  137.4 70.0 %fusion.5 = f32[1,1024]{1,0:T(1,128)S(1)} fusion(f32[16384,1]{0,1:T(1,128)S(1)} %bitcast.15, f32[1024,16384]{1,0:T(8,128)} %get-tuple-element.8, f32[1024]{0:T(1024)S(1)} %pmax.7), kind=kOutput, calls=%fused_computation.19 | convolution fusion | flops 234881024 | bytes 67182592 | tf_op jit(solution)/shard_map/dot_general | solution.py:42
  207.3 9.0 %psum.22 = f32[1024]{0:T(1024)S(1)} all-reduce(f32[1024]{0:T(1024)S(1)} %bitcast.23), channel_id=1, replica_groups=mesh['docs'=8,'protos'=4] {'protos'}, use_global_device_ids=true, to_apply=%region_4.0 | all-reduce | flops 1024 | bytes 8192 | tf_op jit(solution)/shard_map/psum | solution.py:48
  216.3 45.9 %fusion.4 = f32[1,16384]{1,0:T(1,128)S(1)} fusion(f32[1024,1]{0,1:T(1,128)S(1)} %bitcast.21, f32[1024,16384]{1,0:T(8,128)} %get-tuple-element.8, f32[1024]{0:T(1024)S(1)} %pmax.7), kind=kOutput, calls=%fused_computation.18 | convolution fusion | flops 234881024 | bytes 67182592 | tf_op jit(solution)/shard_map/dot_general | solution.py:30
  262.2 0.0 collective-permute-start.3
  262.2 1.3 collective-permute-done.3
  263.5 1.6 collective-permute-start.4
  265.2 2.7 collective-permute-done.4
  267.9 3.0 collective-permute-start.5
  270.8 2.6 collective-permute-done.5
  273.4 0.7 multiply_log_fusion
  274.1 69.5 %fusion.3 = f32[1,1024]{1,0:T(1,128)S(1)} fusion(f32[16384,1]{0,1:T(1,128)S(1)} %bitcast.16, f32[1024,16384]{1,0:T(8,128)} %get-tuple-element.8, f32[1024]{0:T(1024)S(1)} %pmax.7), kind=kOutput, calls=%fused_computation.17 | convolution fusion | flops 234881024 | bytes 67182592 | tf_op jit(solution)/shard_map/dot_general | solution.py:42
  343.6 8.0 %psum.23 = f32[1024]{0:T(1024)S(1)} all-reduce(f32[1024]{0:T(1024)S(1)} %bitcast.24), channel_id=1, replica_groups=mesh['docs'=8,'protos'=4] {'protos'}, use_global_device_ids=true, to_apply=%region_5.0 | all-reduce | flops 1024 | bytes 8192 | tf_op jit(solution)/shard_map/psum | solution.py:48
  351.6 0.6 multiply_log_fusion.1
  352.3 40.1 %fusion = f32[16384,512]{1,0:T(8,128)} fusion(bf16[1024,512]{1,0:T(8,128)(2,1)S(1)} %copy-done, f32[16384]{0:T(1024)S(1)} %get-tuple-element.4, f32[1024]{0:T(1024)S(1)} %get-tuple-element.6, f32[1024,16384]{1,0:T(8,128)} %get-tuple-element.8, f32[1024]{0:T(1024)S(1)} %pmax.7), kind=kOutput, calls=%fused_computation.3 | convolution fusion | flops 17263755264 | bytes 101785600 | tf_op jit(solution)/shard_map/dot_general | solution.py:57
  392.3 0.0 reduce-scatter.2.cloned.1.call-update
  392.3 327.3 %reduce-scatter.2.cloned.1.call-done = f32[2048,512]{1,0:T(8,128)} async-done(((f32[16384,512]{1,0:T(8,128)}), f32[2048,512]{1,0:T(8,128)}) %reduce-scatter.2.cloned.1.call-update) | async-done | bytes 4194320 | tf_op jit(solution)/shard_map/reduce_scatter | solution.py:56
  719.7 2.5 multiply_reduce_fusion.1
  722.2 3.8 multiply_convert_fusion.2
  (8 shorter events, 0.1 us)
Async XLA Ops:
  7.2 1.2 copy-start
  7.2 712.5 %reduce-scatter.2.cloned.1.call-start = ((), (), s32[]{:S(2)}) async-start(), calls=%async_computation.1 | async-start | bytes 37748736 | tf_op jit(solution)/shard_map/reduce_scatter | solution.py:56
  126.5 1.3 collective-permute-start
  127.8 4.3 collective-permute-start.1
  132.1 5.2 collective-permute-start.2
  262.2 1.3 collective-permute-start.3
  263.5 4.3 collective-permute-start.4
  267.9 5.6 collective-permute-start.5
Sparse Core Ops, SparseCore 0:
  392.5 327.1 reduce-scatter.1
